TPU v7x, 32 devices: a whole 2x2x4 slice. The times are simulated.
32 devices in a mesh: grid: 2 (over x), rank: 4 (over y, core), term: 4 (over z).
Axes of the slice: x: 2, y: 2, z: 4, core: 2. Of those that a mesh axis runs over, the one named last changes fastest.
Arguments:
- rhs: float32 [128, 4, 256], P('rank', 'grid')
- coef: float32 [12, 4, 256], P('term', 'grid'), may hold values from 0.03 to 0.3
- env: float32 [12, 128, 128], P('term', 'rank'), as said below
Outputs:
- solution: float32 [128, 4, 256], P('rank', 'grid')
- residual: float32 [128, 4, 256], P('rank', 'grid')
Inputs may be any that keep to these rules, and one draw needn't show every extreme that they name: env[k] is a symmetric matrix for every k.
All inputs are finite; a program needn't handle non-finite values.
Results may differ from a plain program's by a relative error of at most 0.0003.
Values sent between devices are 32-bit elements; how exact they have to be, the bound alone decides.
A program may use at most 64 MiB of HBM per device.

v0:
```python
import jax
import jax.numpy as jnp
from jax import lax
from jax.sharding import PartitionSpec as P

ITERS = 4


def padded_2(block, sides, width):
    for axis, dim in sides:
        count = lax.axis_size(axis)
        forward = [(i, i + 1) for i in range(count - 1)]
        backward = [(target, source) for source, target in forward]
        low = lax.ppermute(
            lax.slice_in_dim(block, block.shape[dim] - width, None, axis=dim), axis, forward
        )
        high = lax.ppermute(lax.slice_in_dim(block, 0, width, axis=dim), axis, backward)
        block = jnp.concatenate([low, block, high], axis=dim)
    return block


def face_weights(padded):
    wide = jnp.pad(padded, ((0, 0), (0, 0), (1, 1)))
    centre = wide[:, 1:-1, 1:-1]
    face_up = 0.5 * (centre + wide[:, 2:, 1:-1])
    face_down = 0.5 * (centre + wide[:, :-2, 1:-1])
    face_right = 0.5 * (centre + wide[:, 1:-1, 2:])
    face_left = 0.5 * (centre + wide[:, 1:-1, :-2])
    return (face_up + face_down + face_right + face_left, face_up, face_down, face_right, face_left)


def apply_faces(field, faces):
    middle = field[..., 1:-1, :]
    sideways = jnp.pad(middle, [(0, 0)] * (middle.ndim - 1) + [(1, 1)])
    total, face_up, face_down, face_right, face_left = faces
    return (
        total * middle
        - face_up * field[..., 2:, :]
        - face_down * field[..., :-2, :]
        - face_right * sideways[..., 2:]
        - face_left * sideways[..., :-2]
    )


def shards(rhs, coef, env):
    coef_padded = padded_2(coef, (("grid", 1),), 1)
    faces = tuple((weights[:, None] for weights in face_weights(coef_padded)))

    def square_sum(vector):
        return lax.psum(jnp.sum(vector * vector), ("grid", "rank"))

    solution = jnp.zeros(rhs.shape, jnp.float32)
    residual = rhs
    direction = rhs
    norm_now = square_sum(residual)
    for step in range(ITERS):
        padded = padded_2(direction, (("grid", 1),), 1)
        stenciled = apply_faces(padded[None], faces)
        image = lax.psum_scatter(
            jnp.einsum("krs,krxy->sxy", env, stenciled, precision=lax.Precision.HIGHEST),
            "rank",
            scatter_dimension=0,
            tiled=True,
        )
        image = lax.psum(image, "term")
        alpha = norm_now / lax.psum(jnp.sum(direction * image), ("grid", "rank"))
        solution = solution + alpha * direction
        residual = residual - alpha * image
        norm_next = square_sum(residual)
        direction = residual + norm_next / norm_now * direction
        norm_now = norm_next
    return (solution, residual)


def solution(mesh):
    placed = (P("rank", "grid", None), P("term", "grid", None), P("term", "rank", None))
    return jax.shard_map(
        shards,
        mesh=mesh,
        in_specs=placed,
        out_specs=(P("rank", "grid", None), P("rank", "grid", None)),
        check_vma=False,
    )
```

profile of v0, /device:TPU:0, one launch (start us, length us, event | category | flops | bytes accessed | tf_op | source)
XLA Modules:
  0.0 443.1 jit_solution(13769848011755938709)
XLA Ops:
  8.0 4.8 %collective-permute-start.1 = (f32[3,1,256]{2,1,0:T(1,128)S(1)}, f32[3,1,256]{2,1,0:T(1,128)S(1)}, u32[]{:S(2)}, u32[]{:S(2)}) collective-permute-start(f32[3,1,256]{2,1,0:T(1,128)S(1)} %get-tuple-element.49), channel_id=1, source_target_pairs={{0,16},{1,17},{2,18},{3,19},{4,20},{5,21},{6,22},{7,23},{8,24},{9,... | collective-permute-start | bytes 9224 | tf_op jit(solution)/shard_map/ppermute | solution.py:14
  15.1 4.5 %collective-permute-start.2 = (f32[32,1,256]{2,1,0:T(1,128)S(1)}, f32[32,1,256]{2,1,0:T(1,128)S(1)}, u32[]{:S(2)}, u32[]{:S(2)}) collective-permute-start(f32[32,1,256]{2,1,0:T(1,128)S(1)} %get-tuple-element.47), channel_id=1, source_target_pairs={{0,16},{1,17},{2,18},{3,19},{4,20},{5,21},{6,22},{7,23},{8,24},{9,... | collective-permute-start | bytes 98312 | tf_op jit(solution)/shard_map/ppermute | solution.py:14
  21.3 4.2 collective-permute-done.3
  29.4 30.5 %all-reduce.27.cloned.1.call-done = f32[128,2,256]{2,1,0:T(2,128)} async-done(((f32[128,2,256]{2,1,0:T(2,128)}), f32[128,2,256]{2,1,0:T(2,128)}) %all-reduce.27.cloned.1.call-update) | async-done | bytes 262160
  61.4 35.5 %all-reduce.19.cloned.1.call-done = f32[32,2,256]{2,1,0:T(2,128)} async-done(((f32[32,2,256]{2,1,0:T(2,128)}), f32[32,2,256]{2,1,0:T(2,128)}) %all-reduce.19.cloned.1.call-update) | async-done | bytes 65552 | tf_op jit(solution)/shard_map/psum | solution.py:65
  98.5 12.5 %all-reduce.9 = (f32[]{:T(128)}, f32[]{:T(128)}) all-reduce(f32[]{:T(128)} %get-tuple-element.5, f32[]{:T(128)} %get-tuple-element.4), channel_id=1, replica_groups=mesh['grid'=2,'rank'=4,'term'=4] {'grid','rank'}, use_global_device_ids=true, to_apply=%region_1.2 | all-reduce | flops 2 | bytes 16 | tf_op jit(solution)/shard_map/psum | solution.py:50
  113.0 12.5 %psum.87 = f32[]{:T(128)} all-reduce(f32[]{:T(128)} %multiply_reduce_fusion.5), channel_id=1, replica_groups=mesh['grid'=2,'rank'=4,'term'=4] {'grid','rank'}, use_global_device_ids=true, to_apply=%region_7.8 | all-reduce | flops 1 | bytes 8 | tf_op jit(solution)/shard_map/psum | solution.py:50
  126.9 3.4 collective-permute-start.4
  131.9 4.2 collective-permute-done.5
  137.8 30.0 %all-reduce.29.cloned.1.call-done = f32[128,2,256]{2,1,0:T(2,128)} async-done(((f32[128,2,256]{2,1,0:T(2,128)}), f32[128,2,256]{2,1,0:T(2,128)}) %all-reduce.29.cloned.1.call-update) | async-done | bytes 262160
  169.3 35.3 %all-reduce.21.cloned.1.call-done = f32[32,2,256]{2,1,0:T(2,128)} async-done(((f32[32,2,256]{2,1,0:T(2,128)}), f32[32,2,256]{2,1,0:T(2,128)}) %all-reduce.21.cloned.1.call-update) | async-done | bytes 65552 | tf_op jit(solution)/shard_map/psum | solution.py:65
  206.2 12.5 %psum.89 = f32[]{:T(128)} all-reduce(f32[]{:T(128)} %multiply_reduce_fusion.4), channel_id=1, replica_groups=mesh['grid'=2,'rank'=4,'term'=4] {'grid','rank'}, use_global_device_ids=true, to_apply=%region_11.12 | all-reduce | flops 1 | bytes 8 | tf_op jit(solution)/shard_map/psum | solution.py:66
  220.7 12.4 %psum.90 = f32[]{:T(128)} all-reduce(f32[]{:T(128)} %get-tuple-element.10), channel_id=1, replica_groups=mesh['grid'=2,'rank'=4,'term'=4] {'grid','rank'}, use_global_device_ids=true, to_apply=%region_13.14 | all-reduce | flops 1 | bytes 8 | tf_op jit(solution)/shard_map/psum | solution.py:50
  234.6 3.4 collective-permute-start.6
  239.6 4.2 collective-permute-done.7
  245.5 30.0 %all-reduce.31.cloned.1.call-done = f32[128,2,256]{2,1,0:T(2,128)} async-done(((f32[128,2,256]{2,1,0:T(2,128)}), f32[128,2,256]{2,1,0:T(2,128)}) %all-reduce.31.cloned.1.call-update) | async-done | bytes 262160
  277.0 35.3 %all-reduce.23.cloned.1.call-done = f32[32,2,256]{2,1,0:T(2,128)} async-done(((f32[32,2,256]{2,1,0:T(2,128)}), f32[32,2,256]{2,1,0:T(2,128)}) %all-reduce.23.cloned.1.call-update) | async-done | bytes 65552 | tf_op jit(solution)/shard_map/psum | solution.py:65
  313.9 12.5 %psum.92 = f32[]{:T(128)} all-reduce(f32[]{:T(128)} %multiply_reduce_fusion.2), channel_id=1, replica_groups=mesh['grid'=2,'rank'=4,'term'=4] {'grid','rank'}, use_global_device_ids=true, to_apply=%region_17.18 | all-reduce | flops 1 | bytes 8 | tf_op jit(solution)/shard_map/psum | solution.py:66
  328.4 12.5 %psum.93 = f32[]{:T(128)} all-reduce(f32[]{:T(128)} %get-tuple-element.8), channel_id=1, replica_groups=mesh['grid'=2,'rank'=4,'term'=4] {'grid','rank'}, use_global_device_ids=true, to_apply=%region_19.20 | all-reduce | flops 1 | bytes 8 | tf_op jit(solution)/shard_map/psum | solution.py:50
  342.3 3.4 collective-permute-start.8
  347.3 4.2 collective-permute-done.9
  353.2 30.0 %all-reduce.33.cloned.1.call-done = f32[128,2,256]{2,1,0:T(2,128)} async-done(((f32[128,2,256]{2,1,0:T(2,128)}), f32[128,2,256]{2,1,0:T(2,128)}) %all-reduce.33.cloned.1.call-update) | async-done | bytes 262160
  384.6 35.5 %all-reduce.25.cloned.1.call-done = f32[32,2,256]{2,1,0:T(2,128)} async-done(((f32[32,2,256]{2,1,0:T(2,128)}), f32[32,2,256]{2,1,0:T(2,128)}) %all-reduce.25.cloned.1.call-update) | async-done | bytes 65552 | tf_op jit(solution)/shard_map/psum | solution.py:65
  421.7 12.5 %psum.95 = f32[]{:T(128)} all-reduce(f32[]{:T(128)} %multiply_reduce_fusion), channel_id=1, replica_groups=mesh['grid'=2,'rank'=4,'term'=4] {'grid','rank'}, use_global_device_ids=true, to_apply=%region_23.24 | all-reduce | flops 1 | bytes 8 | tf_op jit(solution)/shard_map/psum | solution.py:66
  (105 shorter events, 32.7 us)
Async XLA Ops:
  7.2 18.8 %copy-start = (f32[3,32,128]{2,1,0:T(8,128)S(1)}, f32[3,32,128]{2,1,0:T(8,128)}, u32[]{:S(2)}) copy-start(f32[3,32,128]{2,1,0:T(8,128)} %param.5) | copy-start | bytes 147460
  7.2 52.7 %all-reduce.27.cloned.1.call-start = ((), (), s32[]{:S(2)}) async-start(), calls=%async_computation.4 | async-start | bytes 524288
  8.0 13.0 %collective-permute-start.1 = (f32[3,1,256]{2,1,0:T(1,128)S(1)}, f32[3,1,256]{2,1,0:T(1,128)S(1)}, u32[]{:S(2)}, u32[]{:S(2)}) collective-permute-start(f32[3,1,256]{2,1,0:T(1,128)S(1)} %get-tuple-element.49), channel_id=1, source_target_pairs={{0,16},{1,17},{2,18},{3,19},{4,20},{5,21},{6,22},{7,23},{8,24},{9,... | collective-permute-start | bytes 9224 | tf_op jit(solution)/shard_map/ppermute | solution.py:14
  12.8 8.2 %collective-permute-start = (f32[3,1,256]{2,1,0:T(1,128)S(1)}, f32[3,1,256]{2,1,0:T(1,128)S(1)}, u32[]{:S(2)}, u32[]{:S(2)}) collective-permute-start(f32[3,1,256]{2,1,0:T(1,128)S(1)} %get-tuple-element.50), channel_id=1, source_target_pairs={{16,0},{17,1},{18,2},{19,3},{20,4},{21,5},{22,6},{23,7},{24,8},{25... | collective-permute-start | bytes 9224 | tf_op jit(solution)/shard_map/ppermute | solution.py:17
  14.1 6.9 %copy-start.6 = (f32[3,2,256]{2,1,0:T(2,128)S(1)}, f32[3,2,256]{2,1,0:T(2,128)}, u32[]{:S(2)}) copy-start(f32[3,2,256]{2,1,0:T(2,128)} %param.4) | copy-start | bytes 18436
  15.1 6.1 %collective-permute-start.2 = (f32[32,1,256]{2,1,0:T(1,128)S(1)}, f32[32,1,256]{2,1,0:T(1,128)S(1)}, u32[]{:S(2)}, u32[]{:S(2)}) collective-permute-start(f32[32,1,256]{2,1,0:T(1,128)S(1)} %get-tuple-element.47), channel_id=1, source_target_pairs={{0,16},{1,17},{2,18},{3,19},{4,20},{5,21},{6,22},{7,23},{8,24},{9,... | collective-permute-start | bytes 98312 | tf_op jit(solution)/shard_map/ppermute | solution.py:14
  19.7 5.8 %collective-permute-start.3 = (f32[32,1,256]{2,1,0:T(1,128)S(1)}, f32[32,1,256]{2,1,0:T(1,128)S(1)}, u32[]{:S(2)}, u32[]{:S(2)}) collective-permute-start(f32[32,1,256]{2,1,0:T(1,128)S(1)} %get-tuple-element.48), channel_id=1, source_target_pairs={{16,0},{17,1},{18,2},{19,3},{20,4},{21,5},{22,6},{23,7},{24,8},{25... | collective-permute-start | bytes 98312 | tf_op jit(solution)/shard_map/ppermute | solution.py:17
  27.4 69.5 %all-reduce.19.cloned.1.call-start = ((), (), s32[]{:S(2)}) async-start(), calls=%async_computation | async-start | bytes 131072 | tf_op jit(solution)/shard_map/psum | solution.py:65
  61.4 106.4 %all-reduce.29.cloned.1.call-start = ((), (), s32[]{:S(2)}) async-start(), calls=%async_computation.5 | async-start | bytes 524288
  96.9 15.4 %copy-start.2 = (f32[32,2,256]{2,1,0:T(2,128)S(1)}, f32[32,2,256]{2,1,0:T(2,128)}, u32[]{:S(2)}) copy-start(f32[32,2,256]{2,1,0:T(2,128)} %all-reduce.19.cloned.1.call-done) | copy-start | bytes 196612
  126.9 4.9 %collective-permute-start.4 = (f32[32,1,256]{2,1,0:T(1,128)S(1)}, f32[32,1,256]{2,1,0:T(1,128)S(1)}, u32[]{:S(2)}, u32[]{:S(2)}) collective-permute-start(f32[32,1,256]{2,1,0:T(1,128)S(1)} %get-tuple-element.43), channel_id=1, source_target_pairs={{0,16},{1,17},{2,18},{3,19},{4,20},{5,21},{6,22},{7,23},{8,24},{9,... | collective-permute-start | bytes 98312 | tf_op jit(solution)/shard_map/ppermute | solution.py:14
  130.3 5.8 %collective-permute-start.5 = (f32[32,1,256]{2,1,0:T(1,128)S(1)}, f32[32,1,256]{2,1,0:T(1,128)S(1)}, u32[]{:S(2)}, u32[]{:S(2)}) collective-permute-start(f32[32,1,256]{2,1,0:T(1,128)S(1)} %get-tuple-element.44), channel_id=1, source_target_pairs={{16,0},{17,1},{18,2},{19,3},{20,4},{21,5},{22,6},{23,7},{24,8},{25... | collective-permute-start | bytes 98312 | tf_op jit(solution)/shard_map/ppermute | solution.py:17
  137.7 66.9 %all-reduce.21.cloned.1.call-start = ((), (), s32[]{:S(2)}) async-start(), calls=%async_computation.1 | async-start | bytes 131072 | tf_op jit(solution)/shard_map/psum | solution.py:65
  169.2 106.2 %all-reduce.31.cloned.1.call-start = ((), (), s32[]{:S(2)}) async-start(), calls=%async_computation.6 | async-start | bytes 524288
  204.6 15.4 %copy-start.4 = (f32[32,2,256]{2,1,0:T(2,128)S(1)}, f32[32,2,256]{2,1,0:T(2,128)}, u32[]{:S(2)}) copy-start(f32[32,2,256]{2,1,0:T(2,128)} %all-reduce.21.cloned.1.call-done) | copy-start | bytes 196612
  234.6 4.9 %collective-permute-start.6 = (f32[32,1,256]{2,1,0:T(1,128)S(1)}, f32[32,1,256]{2,1,0:T(1,128)S(1)}, u32[]{:S(2)}, u32[]{:S(2)}) collective-permute-start(f32[32,1,256]{2,1,0:T(1,128)S(1)} %get-tuple-element.39), channel_id=1, source_target_pairs={{0,16},{1,17},{2,18},{3,19},{4,20},{5,21},{6,22},{7,23},{8,24},{9,... | collective-permute-start | bytes 98312 | tf_op jit(solution)/shard_map/ppermute | solution.py:14
  238.0 5.8 %collective-permute-start.7 = (f32[32,1,256]{2,1,0:T(1,128)S(1)}, f32[32,1,256]{2,1,0:T(1,128)S(1)}, u32[]{:S(2)}, u32[]{:S(2)}) collective-permute-start(f32[32,1,256]{2,1,0:T(1,128)S(1)} %get-tuple-element.40), channel_id=1, source_target_pairs={{16,0},{17,1},{18,2},{19,3},{20,4},{21,5},{22,6},{23,7},{24,8},{25... | collective-permute-start | bytes 98312 | tf_op jit(solution)/shard_map/ppermute | solution.py:17
  245.4 66.9 %all-reduce.23.cloned.1.call-start = ((), (), s32[]{:S(2)}) async-start(), calls=%async_computation.2 | async-start | bytes 131072 | tf_op jit(solution)/shard_map/psum | solution.py:65
  276.9 106.2 %all-reduce.33.cloned.1.call-start = ((), (), s32[]{:S(2)}) async-start(), calls=%async_computation.7 | async-start | bytes 524288
  312.3 15.4 %copy-start.3 = (f32[32,2,256]{2,1,0:T(2,128)S(1)}, f32[32,2,256]{2,1,0:T(2,128)}, u32[]{:S(2)}) copy-start(f32[32,2,256]{2,1,0:T(2,128)} %all-reduce.23.cloned.1.call-done) | copy-start | bytes 196612
  342.3 4.9 %collective-permute-start.8 = (f32[32,1,256]{2,1,0:T(1,128)S(1)}, f32[32,1,256]{2,1,0:T(1,128)S(1)}, u32[]{:S(2)}, u32[]{:S(2)}) collective-permute-start(f32[32,1,256]{2,1,0:T(1,128)S(1)} %get-tuple-element.35), channel_id=1, source_target_pairs={{0,16},{1,17},{2,18},{3,19},{4,20},{5,21},{6,22},{7,23},{8,24},{9,... | collective-permute-start | bytes 98312 | tf_op jit(solution)/shard_map/ppermute | solution.py:14
  345.7 5.8 %collective-permute-start.9 = (f32[32,1,256]{2,1,0:T(1,128)S(1)}, f32[32,1,256]{2,1,0:T(1,128)S(1)}, u32[]{:S(2)}, u32[]{:S(2)}) collective-permute-start(f32[32,1,256]{2,1,0:T(1,128)S(1)} %get-tuple-element.36), channel_id=1, source_target_pairs={{16,0},{17,1},{18,2},{19,3},{20,4},{21,5},{22,6},{23,7},{24,8},{25... | collective-permute-start | bytes 98312 | tf_op jit(solution)/shard_map/ppermute | solution.py:17
  353.1 67.0 %all-reduce.25.cloned.1.call-start = ((), (), s32[]{:S(2)}) async-start(), calls=%async_computation.3 | async-start | bytes 131072 | tf_op jit(solution)/shard_map/psum | solution.py:65
  420.1 15.4 %copy-start.5 = (f32[32,2,256]{2,1,0:T(2,128)S(1)}, f32[32,2,256]{2,1,0:T(2,128)}, u32[]{:S(2)}) copy-start(f32[32,2,256]{2,1,0:T(2,128)} %all-reduce.25.cloned.1.call-done) | copy-start | bytes 196612
  (2 other events, 5.0 us)
Sparse Core Ops, SparseCore 0:
  27.6 32.2 all-reduce.26
  62.9 33.9 all-reduce.18
  137.9 29.8 all-reduce.28
  170.6 33.9 all-reduce.20
  245.5 29.8 all-reduce.30
  278.3 33.9 all-reduce.22
  353.2 29.8 all-reduce.32
  386.1 33.9 all-reduce.24
where the time goes:
time: 444 us; the launch traced here: 443 us
  waiting for transfers between devices  280 us (63%)
  blocking collectives  87.3 us (20%)
  starting transfers between devices  26.2 us (6%)
  between operations  24.8 us (6%)
  local copies, waits for them, and re-layouts  13.1 us (3%)
  other arithmetic  9.37 us (2%)
    psum x4, waiting for transfers between devices, shards(): image = lax.psum(image, 'term')  142 us
    unnamed x12, waiting for transfers between devices  121 us
    psum x4, blocking collectives, square_sum(): return lax.psum(jnp.sum(vector * vector), ('grid', 'rank'))  49.9 us
    psum x3, blocking collectives, shards(): alpha = norm_now / lax.psum(jnp.sum(direction * image), ('grid', 'rank'))  37.4 us
    ppermute x5, starting transfers between devices, padded_2(): lax.ppermute(lax.slice_in_dim(block, block.shape[dim] - width, None, axis...  19.4 us
    ppermute x5, waiting for transfers between devices, padded_2(): lax.ppermute(lax.slice_in_dim(block, 0, width, axis=dim), axis, backward)  16.9 us
  transfers between devices with their start and end apart: 18, of which 15 were waited for; matrix products, arithmetic and copies ran while one was open for 0% of the time, Pallas kernels for 0%

commit v1 on v0

--- a/solution.py
+++ b/solution.py
@@ -62,7 +62,7 @@
             scatter_dimension=0,
             tiled=True,
         )
-        image = lax.psum(image, "term")
+        image = jnp.sum(lax.all_gather(image, "term"), axis=0)
         alpha = norm_now / lax.psum(jnp.sum(direction * image), ("grid", "rank"))
         solution = solution + alpha * direction
         residual = residual - alpha * image

time: 444 us -> 355 us (0.80)
  waiting for transfers between devices: 280 us -> 141 us
  blocking collectives: 87.3 us -> 142 us
    psum x4 -> x0, waiting for transfers between devices: 142 us -> none  [shards(): image = lax.psum(image, 'term')]
    all_gather x0 -> x4, blocking collectives: none -> 55.5 us  [shards(): image = jnp.sum(lax.all_gather(image, 'term'), axis=0)]
    unnamed x12 -> x8, waiting for transfers between devices: 121 us -> 124 us
  transfers between devices with their start and end apart: 18 -> 14, of which waited for: 15 -> 11; matrix products, arithmetic and copies ran while one was open for 0% -> 1% of each run, Pallas kernels for 0% -> 0%
where the time goes in v1:
time: 355 us; the launch traced here: 354 us
  blocking collectives  142 us (40%)
  waiting for transfers between devices  141 us (40%)
  starting transfers between devices  26.2 us (7%)
  between operations  24.2 us (7%)
  local copies, waits for them, and re-layouts  11.8 us (3%)
  other arithmetic  5.81 us (2%)
    unnamed x8, waiting for transfers between devices  124 us
    all_gather x4, blocking collectives, shards(): image = jnp.sum(lax.all_gather(image, 'term'), axis=0)  55.5 us
    psum x4, blocking collectives, square_sum(): return lax.psum(jnp.sum(vector * vector), ('grid', 'rank'))  49.6 us
    psum x3, blocking collectives, shards(): alpha = norm_now / lax.psum(jnp.sum(direction * image), ('grid', 'rank'))  37.2 us
    ppermute x5, starting transfers between devices, padded_2(): lax.ppermute(lax.slice_in_dim(block, block.shape[dim] - width, None, axis...  19.5 us
    ppermute x5, waiting for transfers between devices, padded_2(): lax.ppermute(lax.slice_in_dim(block, 0, width, axis=dim), axis, backward)  16.9 us
  transfers between devices with their start and end apart: 14, of which 11 were waited for; matrix products, arithmetic and copies ran while one was open for 1% of the time, Pallas kernels for 0%

profile of v1, /device:TPU:0, one launch (start us, length us, event | category | flops | bytes accessed | tf_op | source)
XLA Modules:
  0.0 354.2 jit_solution(17296107138982622128)
XLA Ops:
  8.0 4.8 %collective-permute-start.1 = (f32[3,1,256]{2,1,0:T(1,128)S(1)}, f32[3,1,256]{2,1,0:T(1,128)S(1)}, u32[]{:S(2)}, u32[]{:S(2)}) collective-permute-start(f32[3,1,256]{2,1,0:T(1,128)S(1)} %get-tuple-element.47), channel_id=1, source_target_pairs={{0,16},{1,17},{2,18},{3,19},{4,20},{5,21},{6,22},{7,23},{8,24},{9,... | collective-permute-start | bytes 9224 | tf_op jit(solution)/shard_map/ppermute | solution.py:14
  15.1 4.5 %collective-permute-start.2 = (f32[32,1,256]{2,1,0:T(1,128)S(1)}, f32[32,1,256]{2,1,0:T(1,128)S(1)}, u32[]{:S(2)}, u32[]{:S(2)}) collective-permute-start(f32[32,1,256]{2,1,0:T(1,128)S(1)} %get-tuple-element.45), channel_id=1, source_target_pairs={{0,16},{1,17},{2,18},{3,19},{4,20},{5,21},{6,22},{7,23},{8,24},{9,... | collective-permute-start | bytes 98312 | tf_op jit(solution)/shard_map/ppermute | solution.py:14
  21.3 4.2 %collective-permute-done.3 = f32[32,1,256]{2,1,0:T(1,128)S(1)} collective-permute-done((f32[32,1,256]{2,1,0:T(1,128)S(1)}, f32[32,1,256]{2,1,0:T(1,128)S(1)}, u32[]{:S(2)}, u32[]{:S(2)}) %collective-permute-start.3) | collective-permute-done | bytes 32800 | tf_op jit(solution)/shard_map/ppermute | solution.py:17
  30.1 29.8 %all-reduce.15.cloned.1.call-done = f32[128,2,256]{2,1,0:T(2,128)} async-done(((f32[128,2,256]{2,1,0:T(2,128)}), f32[128,2,256]{2,1,0:T(2,128)}) %all-reduce.15.cloned.1.call-update) | async-done | bytes 262160
  60.7 13.9 %all-gather = f32[128,2,256]{2,1,0:T(2,128)S(1)} all-gather(f32[32,2,256]{2,1,0:T(2,128)S(1)} %constant_dynamic-slice_fusion.3), channel_id=2, replica_groups=mesh['grid'=2,'rank'=4,'term'=4] {'term'}, dimensions={0}, use_global_device_ids=true | all-gather | bytes 327680 | tf_op jit(solution)/shard_map/all_gather | solution.py:65
  75.3 12.4 %all-reduce.9 = (f32[]{:T(128)}, f32[]{:T(128)}) all-reduce(f32[]{:T(128)} %multiply_reduce_fusion.7, f32[]{:T(128)} %multiply_reduce_fusion.6), channel_id=1, replica_groups=mesh['grid'=2,'rank'=4,'term'=4] {'grid','rank'}, use_global_device_ids=true, to_apply=%region_1.2 | all-reduce | flops 2 | bytes 16 | tf_op jit(solution)/shard_map/psum | solution.py:50
  89.7 12.4 %psum.58 = f32[]{:T(128)} all-reduce(f32[]{:T(128)} %multiply_reduce_fusion.5), channel_id=1, replica_groups=mesh['grid'=2,'rank'=4,'term'=4] {'grid','rank'}, use_global_device_ids=true, to_apply=%region_7.8 | all-reduce | flops 1 | bytes 8 | tf_op jit(solution)/shard_map/psum | solution.py:50
  103.5 3.4 collective-permute-start.4
  108.5 4.2 %collective-permute-done.5 = f32[32,1,256]{2,0,1:T(8,128)S(1)} collective-permute-done((f32[32,1,256]{2,0,1:T(8,128)S(1)}, f32[32,1,256]{2,0,1:T(8,128)S(1)}, u32[]{:S(2)}, u32[]{:S(2)}) %collective-permute-start.5) | collective-permute-done | bytes 32800 | tf_op jit(solution)/shard_map/ppermute | solution.py:17
  114.4 31.2 %all-reduce.17.cloned.1.call-done = f32[128,2,256]{2,1,0:T(2,128)} async-done(((f32[128,2,256]{2,1,0:T(2,128)}), f32[128,2,256]{2,1,0:T(2,128)}) %all-reduce.17.cloned.1.call-update) | async-done | bytes 262160
  146.5 13.9 %all-gather.1 = f32[128,2,256]{2,1,0:T(2,128)S(1)} all-gather(f32[32,2,256]{2,1,0:T(2,128)S(1)} %constant_dynamic-slice_fusion.2), channel_id=3, replica_groups=mesh['grid'=2,'rank'=4,'term'=4] {'term'}, dimensions={0}, use_global_device_ids=true | all-gather | bytes 327680 | tf_op jit(solution)/shard_map/all_gather | solution.py:65
  161.1 12.4 %psum.59 = f32[]{:T(128)} all-reduce(f32[]{:T(128)} %multiply_reduce_fusion.4), channel_id=1, replica_groups=mesh['grid'=2,'rank'=4,'term'=4] {'grid','rank'}, use_global_device_ids=true, to_apply=%region_11.12 | all-reduce | flops 1 | bytes 8 | tf_op jit(solution)/shard_map/psum | solution.py:66
  175.5 12.4 %psum.60 = f32[]{:T(128)} all-reduce(f32[]{:T(128)} %get-tuple-element.8), channel_id=1, replica_groups=mesh['grid'=2,'rank'=4,'term'=4] {'grid','rank'}, use_global_device_ids=true, to_apply=%region_13.14 | all-reduce | flops 1 | bytes 8 | tf_op jit(solution)/shard_map/psum | solution.py:50
  189.2 3.4 collective-permute-start.6
  194.2 4.2 %collective-permute-done.7 = f32[32,1,256]{2,0,1:T(8,128)S(1)} collective-permute-done((f32[32,1,256]{2,0,1:T(8,128)S(1)}, f32[32,1,256]{2,0,1:T(8,128)S(1)}, u32[]{:S(2)}, u32[]{:S(2)}) %collective-permute-start.7) | collective-permute-done | bytes 32800 | tf_op jit(solution)/shard_map/ppermute | solution.py:17
  200.1 31.2 %all-reduce.19.cloned.1.call-done = f32[128,2,256]{2,1,0:T(2,128)} async-done(((f32[128,2,256]{2,1,0:T(2,128)}), f32[128,2,256]{2,1,0:T(2,128)}) %all-reduce.19.cloned.1.call-update) | async-done | bytes 262160
  232.2 13.9 %all-gather.2 = f32[128,2,256]{2,1,0:T(2,128)S(1)} all-gather(f32[32,2,256]{2,1,0:T(2,128)S(1)} %constant_dynamic-slice_fusion.1), channel_id=4, replica_groups=mesh['grid'=2,'rank'=4,'term'=4] {'term'}, dimensions={0}, use_global_device_ids=true | all-gather | bytes 327680 | tf_op jit(solution)/shard_map/all_gather | solution.py:65
  246.8 12.4 %psum.61 = f32[]{:T(128)} all-reduce(f32[]{:T(128)} %multiply_reduce_fusion.2), channel_id=1, replica_groups=mesh['grid'=2,'rank'=4,'term'=4] {'grid','rank'}, use_global_device_ids=true, to_apply=%region_17.18 | all-reduce | flops 1 | bytes 8 | tf_op jit(solution)/shard_map/psum | solution.py:66
  261.2 12.4 %psum.62 = f32[]{:T(128)} all-reduce(f32[]{:T(128)} %get-tuple-element.6), channel_id=1, replica_groups=mesh['grid'=2,'rank'=4,'term'=4] {'grid','rank'}, use_global_device_ids=true, to_apply=%region_19.20 | all-reduce | flops 1 | bytes 8 | tf_op jit(solution)/shard_map/psum | solution.py:50
  275.0 3.4 collective-permute-start.8
  279.9 4.2 %collective-permute-done.9 = f32[32,1,256]{2,0,1:T(8,128)S(1)} collective-permute-done((f32[32,1,256]{2,0,1:T(8,128)S(1)}, f32[32,1,256]{2,0,1:T(8,128)S(1)}, u32[]{:S(2)}, u32[]{:S(2)}) %collective-permute-start.9) | collective-permute-done | bytes 32800 | tf_op jit(solution)/shard_map/ppermute | solution.py:17
  285.8 31.3 %all-reduce.21.cloned.1.call-done = f32[128,2,256]{2,1,0:T(2,128)} async-done(((f32[128,2,256]{2,1,0:T(2,128)}), f32[128,2,256]{2,1,0:T(2,128)}) %all-reduce.21.cloned.1.call-update) | async-done | bytes 262160
  317.9 13.9 %all-gather.3 = f32[128,2,256]{2,1,0:T(2,128)S(1)} all-gather(f32[32,2,256]{2,1,0:T(2,128)S(1)} %constant_dynamic-slice_fusion), channel_id=5, replica_groups=mesh['grid'=2,'rank'=4,'term'=4] {'term'}, dimensions={0}, use_global_device_ids=true | all-gather | bytes 327680 | tf_op jit(solution)/shard_map/all_gather | solution.py:65
  332.5 12.4 %psum.63 = f32[]{:T(128)} all-reduce(f32[]{:T(128)} %multiply_reduce_fusion), channel_id=1, replica_groups=mesh['grid'=2,'rank'=4,'term'=4] {'grid','rank'}, use_global_device_ids=true, to_apply=%region_23.24 | all-reduce | flops 1 | bytes 8 | tf_op jit(solution)/shard_map/psum | solution.py:66
  (87 shorter events, 27.6 us)
Async XLA Ops:
  7.2 18.8 %copy-start = (f32[3,32,128]{2,1,0:T(8,128)S(1)}, f32[3,32,128]{2,1,0:T(8,128)}, u32[]{:S(2)}) copy-start(f32[3,32,128]{2,1,0:T(8,128)} %param.5) | copy-start | bytes 147460
  7.2 52.7 %all-reduce.15.cloned.1.call-start = ((), (), s32[]{:S(2)}) async-start(), calls=%async_computation | async-start | bytes 524288
  8.0 13.0 %collective-permute-start.1 = (f32[3,1,256]{2,1,0:T(1,128)S(1)}, f32[3,1,256]{2,1,0:T(1,128)S(1)}, u32[]{:S(2)}, u32[]{:S(2)}) collective-permute-start(f32[3,1,256]{2,1,0:T(1,128)S(1)} %get-tuple-element.47), channel_id=1, source_target_pairs={{0,16},{1,17},{2,18},{3,19},{4,20},{5,21},{6,22},{7,23},{8,24},{9,... | collective-permute-start | bytes 9224 | tf_op jit(solution)/shard_map/ppermute | solution.py:14
  12.8 8.2 %collective-permute-start = (f32[3,1,256]{2,1,0:T(1,128)S(1)}, f32[3,1,256]{2,1,0:T(1,128)S(1)}, u32[]{:S(2)}, u32[]{:S(2)}) collective-permute-start(f32[3,1,256]{2,1,0:T(1,128)S(1)} %get-tuple-element.48), channel_id=1, source_target_pairs={{16,0},{17,1},{18,2},{19,3},{20,4},{21,5},{22,6},{23,7},{24,8},{25... | collective-permute-start | bytes 9224 | tf_op jit(solution)/shard_map/ppermute | solution.py:17
  14.1 6.9 %copy-start.2 = (f32[3,2,256]{2,1,0:T(2,128)S(1)}, f32[3,2,256]{2,1,0:T(2,128)}, u32[]{:S(2)}) copy-start(f32[3,2,256]{2,1,0:T(2,128)} %param.4) | copy-start | bytes 18436
  15.1 6.1 %collective-permute-start.2 = (f32[32,1,256]{2,1,0:T(1,128)S(1)}, f32[32,1,256]{2,1,0:T(1,128)S(1)}, u32[]{:S(2)}, u32[]{:S(2)}) collective-permute-start(f32[32,1,256]{2,1,0:T(1,128)S(1)} %get-tuple-element.45), channel_id=1, source_target_pairs={{0,16},{1,17},{2,18},{3,19},{4,20},{5,21},{6,22},{7,23},{8,24},{9,... | collective-permute-start | bytes 98312 | tf_op jit(solution)/shard_map/ppermute | solution.py:14
  19.7 5.8 %collective-permute-start.3 = (f32[32,1,256]{2,1,0:T(1,128)S(1)}, f32[32,1,256]{2,1,0:T(1,128)S(1)}, u32[]{:S(2)}, u32[]{:S(2)}) collective-permute-start(f32[32,1,256]{2,1,0:T(1,128)S(1)} %get-tuple-element.46), channel_id=1, source_target_pairs={{16,0},{17,1},{18,2},{19,3},{20,4},{21,5},{22,6},{23,7},{24,8},{25... | collective-permute-start | bytes 98312 | tf_op jit(solution)/shard_map/ppermute | solution.py:17
  21.1 4.4 %copy-start.1 = (f32[32,2,256]{2,1,0:T(2,128)S(1)}, f32[32,2,256]{2,1,0:T(2,128)}, u32[]{:S(2)}) copy-start(f32[32,2,256]{2,1,0:T(2,128)} %param.3) | copy-start | bytes 196612
  27.4 118.2 %all-reduce.17.cloned.1.call-start = ((), (), s32[]{:S(2)}) async-start(), calls=%async_computation.1 | async-start | bytes 524288
  27.5 0.7 copy-start.3
  103.5 5.0 %collective-permute-start.4 = (f32[32,1,256]{2,0,1:T(8,128)S(1)}, f32[32,1,256]{2,0,1:T(8,128)S(1)}, u32[]{:S(2)}, u32[]{:S(2)}) collective-permute-start(f32[32,1,256]{2,0,1:T(8,128)S(1)} %get-tuple-element.41), channel_id=1, source_target_pairs={{0,16},{1,17},{2,18},{3,19},{4,20},{5,21},{6,22},{7,23},{8,24},{9,... | collective-permute-start | bytes 98312 | tf_op jit(solution)/shard_map/ppermute | solution.py:14
  106.9 5.8 %collective-permute-start.5 = (f32[32,1,256]{2,0,1:T(8,128)S(1)}, f32[32,1,256]{2,0,1:T(8,128)S(1)}, u32[]{:S(2)}, u32[]{:S(2)}) collective-permute-start(f32[32,1,256]{2,0,1:T(8,128)S(1)} %get-tuple-element.42), channel_id=1, source_target_pairs={{16,0},{17,1},{18,2},{19,3},{20,4},{21,5},{22,6},{23,7},{24,8},{25... | collective-permute-start | bytes 98312 | tf_op jit(solution)/shard_map/ppermute | solution.py:17
  114.3 117.0 %all-reduce.19.cloned.1.call-start = ((), (), s32[]{:S(2)}) async-start(), calls=%async_computation.2 | async-start | bytes 524288
  189.2 5.0 %collective-permute-start.6 = (f32[32,1,256]{2,0,1:T(8,128)S(1)}, f32[32,1,256]{2,0,1:T(8,128)S(1)}, u32[]{:S(2)}, u32[]{:S(2)}) collective-permute-start(f32[32,1,256]{2,0,1:T(8,128)S(1)} %get-tuple-element.37), channel_id=1, source_target_pairs={{0,16},{1,17},{2,18},{3,19},{4,20},{5,21},{6,22},{7,23},{8,24},{9,... | collective-permute-start | bytes 98312 | tf_op jit(solution)/shard_map/ppermute | solution.py:14
  192.6 5.8 %collective-permute-start.7 = (f32[32,1,256]{2,0,1:T(8,128)S(1)}, f32[32,1,256]{2,0,1:T(8,128)S(1)}, u32[]{:S(2)}, u32[]{:S(2)}) collective-permute-start(f32[32,1,256]{2,0,1:T(8,128)S(1)} %get-tuple-element.38), channel_id=1, source_target_pairs={{16,0},{17,1},{18,2},{19,3},{20,4},{21,5},{22,6},{23,7},{24,8},{25... | collective-permute-start | bytes 98312 | tf_op jit(solution)/shard_map/ppermute | solution.py:17
  200.1 117.0 %all-reduce.21.cloned.1.call-start = ((), (), s32[]{:S(2)}) async-start(), calls=%async_computation.3 | async-start | bytes 524288
  275.0 5.0 %collective-permute-start.8 = (f32[32,1,256]{2,0,1:T(8,128)S(1)}, f32[32,1,256]{2,0,1:T(8,128)S(1)}, u32[]{:S(2)}, u32[]{:S(2)}) collective-permute-start(f32[32,1,256]{2,0,1:T(8,128)S(1)} %get-tuple-element.33), channel_id=1, source_target_pairs={{0,16},{1,17},{2,18},{3,19},{4,20},{5,21},{6,22},{7,23},{8,24},{9,... | collective-permute-start | bytes 98312 | tf_op jit(solution)/shard_map/ppermute | solution.py:14
  278.4 5.8 %collective-permute-start.9 = (f32[32,1,256]{2,0,1:T(8,128)S(1)}, f32[32,1,256]{2,0,1:T(8,128)S(1)}, u32[]{:S(2)}, u32[]{:S(2)}) collective-permute-start(f32[32,1,256]{2,0,1:T(8,128)S(1)} %get-tuple-element.34), channel_id=1, source_target_pairs={{16,0},{17,1},{18,2},{19,3},{20,4},{21,5},{22,6},{23,7},{24,8},{25... | collective-permute-start | bytes 98312 | tf_op jit(solution)/shard_map/ppermute | solution.py:17
Sparse Core Ops, SparseCore 0:
  27.6 32.2 all-reduce.14
  114.5 31.1 all-reduce.16
  200.2 31.0 all-reduce.18
  285.9 31.1 all-reduce.20
